TPU v7x, 32 devices: a whole 2x2x4 slice. The times are simulated.
32 devices in a mesh: row: 4 (over z), col: 8 (over y, x, core).
Axes of the slice: x: 2, y: 2, z: 4, core: 2. Of those that a mesh axis runs over, the one named last changes fastest.
Arguments:
- adjusted_rows: bfloat16 [8192, 29568], P(('row', 'col')), may hold values from -5 to 5
- base_weight: bfloat16 [8192, 29568], P('row', 'col'), may hold values from -5 to 5
- range_test: bfloat16 [29568, 384], P('col'), may hold values from -0.03125 to 0.03125
- corange_test: bfloat16 [384, 8192], P(None, 'row'), may hold values from -0.0625 to 0.0625
- core_left: bfloat16 [768, 8192], P(None, 'row'), may hold values from -0.0625 to 0.0625
- core_right: bfloat16 [768, 29568], P(None, 'col'), may hold values from -1 to 1
Outputs:
- range_sketch: float32 [8192, 384], P('row')
- corange_sketch: float32 [384, 29568], P(None, 'col')
- core_solution: float32 [384, 768], P(None, 'col')
All inputs are finite; a program needn't handle non-finite values.
Results may differ from a plain program's by a relative error of at most 0.0066.
Values may be sent and summed in bfloat16 or wider, within the bound.
A program may use at most 192 MiB of HBM per device.

v0:
```python
import jax
import jax.numpy as jnp
from jax import lax
from jax.sharding import PartitionSpec as P

S = 768


def local(adjusted_rows, base_weight, range_test, corange_test, core_left, core_right):
    highest = lax.Precision.HIGHEST
    adjusted_block = lax.all_to_all(adjusted_rows, "col", split_axis=1, concat_axis=0, tiled=True)
    difference = (adjusted_block.astype(jnp.float32) - base_weight.astype(jnp.float32)).astype(
        jnp.bfloat16
    )
    range_part = jnp.dot(difference, range_test, preferred_element_type=jnp.float32)
    range_sketch = lax.psum(range_part, "col")
    corange_part = jnp.dot(corange_test, difference, preferred_element_type=jnp.float32)
    corange_sketch = lax.psum(corange_part, "row")
    left_float = core_left.astype(jnp.float32)
    projected_part = jnp.dot(left_float, range_sketch, precision=highest)
    share_width = S // lax.axis_size("col")
    projected = lax.psum(projected_part, "row")
    left_product = jnp.dot(core_left, difference, preferred_element_type=jnp.float32)
    partial_value = jnp.dot(left_product, core_right.astype(jnp.float32).T, precision=highest)
    core_sketch = lax.psum(partial_value, ("row", "col"))
    own_columns = lax.dynamic_slice_in_dim(
        core_sketch, lax.axis_index("col") * share_width, share_width, 1
    )
    gram_matrix = jnp.dot(projected.T, projected, precision=highest)
    right_hand = jnp.dot(projected.T, own_columns, precision=highest)
    factor = jnp.linalg.cholesky(gram_matrix)
    halfway = lax.linalg.triangular_solve(factor, right_hand, left_side=True, lower=True)
    core_solution = lax.linalg.triangular_solve(
        factor, halfway, left_side=True, lower=True, transpose_a=True
    )
    return (range_sketch, corange_sketch, core_solution)


def solution(mesh):
    in_specs = (
        P(("row", "col"), None),
        P("row", "col"),
        P("col", None),
        P(None, "row"),
        P(None, "row"),
        P(None, "col"),
    )
    out_specs = (P("row", None), P(None, "col"), P(None, "col"))
    return jax.shard_map(local, mesh=mesh, in_specs=in_specs, out_specs=out_specs, check_vma=False)
```

profile of v0, /device:TPU:0, one launch (start us, length us, event | category | flops | bytes accessed | tf_op | source)
XLA Modules:
  0.0 764.8 jit_solution(4996886809398018874)
XLA Ops:
  7.2 20.6 %copy.13 = bf16[256,29568]{0,1:T(8,128)(2,1)} copy(bf16[256,29568]{1,0:T(8,128)(2,1)} %param.6) | data formatting | bytes 30277632 | tf_op args[0]
  27.8 5.6 all-to-all-start
  33.4 19.0 %copy.15 = bf16[2048,3696]{1,0:T(8,128)(2,1)} copy(bf16[2048,3696]{0,1:T(8,128)(2,1)} %param.7) | data formatting | bytes 30277632 | tf_op args[1]
  52.4 147.9 %all-to-all-done = bf16[256,8,3696]{0,2,1:T(8,128)(2,1)} async-done(((bf16[256,8,3696]{0,2,1:T(8,128)(2,1)}), bf16[256,8,3696]{0,2,1:T(8,128)(2,1)}, u32[]{:S(2)}, u32[]{:S(2)}) %all-to-all-start) | async-done | bytes 15138848 | tf_op jit(solution)/shard_map/all_to_all | solution.py:11
  200.4 16.8 %convert_bitcast_fusion = f32[8,256,3696]{1,2,0:T(8,128)} fusion(bf16[256,8,3696]{0,2,1:T(8,128)(2,1)} %all-to-all-done), kind=kLoop, calls=%fused_computation.4 | loop fusion | flops 7569408 | bytes 45416448 | tf_op jit(solution)/shard_map/convert_element_type | solution.py:12
  217.2 30.1 %copy.14 = f32[8,256,3696]{2,1,0:T(8,128)} copy(f32[8,256,3696]{1,2,0:T(8,128)} %convert_bitcast_fusion) | data formatting | bytes 60555264 | tf_op jit(solution)/shard_map/convert_element_type | solution.py:12
  247.3 14.8 %fusion = bf16[2048,3696]{1,0:T(8,128)(2,1)S(1)} fusion(f32[8,256,3696]{2,1,0:T(8,128)} %copy.14, bf16[2048,3696]{1,0:T(8,128)(2,1)} %copy.15), kind=kLoop, calls=%fused_computation.3 | loop fusion | flops 22708224 | bytes 60555264 | tf_op jit(solution)/shard_map/convert_element_type | solution.py:12
  262.1 5.3 copy-done.1
  267.4 10.1 %fusion.32 = f32[2048,384]{1,0:T(8,128)} fusion(bf16[2048,3696]{1,0:T(8,128)(2,1)S(1)} %fusion, bf16[3696,384]{1,0:T(8,128)(2,1)S(1)} %copy-done.4), kind=kOutput, calls=%fused_computation.66 | convolution fusion | flops 5813305344 | bytes 21123072 | tf_op jit(solution)/shard_map/dot_general | solution.py:15
  278.2 13.8 %convolution_bitcast_fusion = f32[384,3696]{0,1:T(8,128)} fusion(bf16[2048,3696]{1,0:T(8,128)(2,1)} %copy-done.1, bf16[384,2048]{1,0:T(8,128)(2,1)} %param.9), kind=kOutput, calls=%fused_computation.5 | convolution fusion | flops 5813305344 | bytes 22388736 | tf_op jit(solution)/shard_map/dot_general | solution.py:17
  292.0 55.5 %all-reduce.6.cloned.1.call-done = f32[2048,384]{1,0:T(8,128)} async-done(((f32[2048,384]{1,0:T(8,128)}), f32[2048,384]{1,0:T(8,128)}) %all-reduce.6.cloned.1.call-update) | async-done | bytes 3145744 | tf_op jit(solution)/shard_map/psum | solution.py:16
  347.4 10.5 %convolution_bitcast_fusion.1 = f32[768,384]{0,1:T(8,128)} fusion(f32[2048,384]{1,0:T(8,128)} %all-reduce.6.cloned.1.call-done, bf16[768,2048]{1,0:T(8,128)(2,1)S(1)} %copy-done), kind=kOutput, calls=%fused_computation.6 | convolution fusion | flops 7247757312 | bytes 7471104 | tf_op jit(solution)/shard_map/dot_general | solution.py:20
  358.2 15.8 %fusion.34 = f32[3696,768]{1,0:T(8,128)S(1)} fusion(bf16[2048,3696]{1,0:T(8,128)(2,1)} %copy-done.1, bf16[768,2048]{1,0:T(8,128)(2,1)S(1)} %copy-done), kind=kOutput, calls=%fused_computation.68 | convolution fusion | flops 11626610688 | bytes 29638656 | tf_op jit(solution)/shard_map/dot_general | solution.py:23
  374.0 18.4 %fusion.35 = f32[768,768]{0,1:T(8,128)} fusion(f32[3696,768]{1,0:T(8,128)S(1)} %fusion.34, bf16[768,3696]{0,1:T(8,128)(2,1)} %param.11), kind=kOutput, calls=%fused_computation.69 | convolution fusion | flops 26159874048 | bytes 19390464 | tf_op jit(solution)/shard_map/dot_general | solution.py:24
  392.4 207.5 %all-reduce.10.cloned.1.call-done = (f32[384,3696]{0,1:T(8,128)}, f32[768,384]{0,1:T(8,128)}) async-done(((f32[384,3696]{0,1:T(8,128)}, f32[768,384]{0,1:T(8,128)}), (f32[384,3696]{0,1:T(8,128)}, f32[768,384]{0,1:T(8,128)})) %all-reduce.10.cloned.1.call-update) | async-done | bytes 6856720 | tf_op jit(solution)/shard_map/psum | solution.py:18
  599.9 4.5 fusion.33
  604.4 2.1 copy.16
  608.7 11.7 %cholesky.77 = f32[128,128]{1,0:T(8,128)S(1)} custom-call(f32[128,128]{1,0:T(8,128)S(1)} %cholesky.192), custom_call_target="Cholesky" | custom-call | tf_op jit(solution)/shard_map/jit(cholesky)/cholesky | solution.py:31
  620.4 9.8 %custom-call.24 = f32[1,128,128]{1,2,0:T(8,128)S(1)} custom-call(f32[1,128,128]{2,1,0:T(8,128)S(1)} %get-tuple-element.29), custom_call_target="InvertDiagBlocksLowerTriangular" | custom-call | tf_op jit(solution)/shard_map/jit(cholesky)/cholesky | solution.py:31
  631.1 1.8 constant_dynamic-update-slice_fusion.2
  634.1 12.0 %cholesky.162 = f32[128,128]{1,0:T(8,128)S(1)} custom-call(f32[128,128]{1,0:T(8,128)S(1)} %cholesky.196), custom_call_target="Cholesky" | custom-call | tf_op jit(solution)/shard_map/jit(cholesky)/cholesky | solution.py:31
  646.7 9.8 %custom-call.25 = f32[1,128,128]{1,2,0:T(8,128)S(1)} custom-call(f32[1,128,128]{2,1,0:T(8,128)S(1)} %get-tuple-element.26), custom_call_target="InvertDiagBlocksLowerTriangular" | custom-call | tf_op jit(solution)/shard_map/jit(cholesky)/cholesky | solution.py:31
  658.7 11.7 %cholesky.181 = f32[128,128]{1,0:T(8,128)S(1)} custom-call(f32[128,128]{1,0:T(8,128)S(1)} %convolution_subtract_fusion.1), custom_call_target="Cholesky" | custom-call | tf_op jit(solution)/shard_map/jit(cholesky)/cholesky | solution.py:31
  674.1 1.9 select_select_fusion
  676.1 10.5 %while.1 = (s32[]{:T(128)}, f32[384,384]{1,0:T(8,128)}, s32[3,2]{0,1:T(2,128)S(1)}, f32[3,128,128]{2,1,0:T(8,128)}, s32[]{:T(128)}) while((s32[]{:T(128)}, f32[384,384]{1,0:T(8,128)}, s32[3,2]{0,1:T(2,128)S(1)}, f32[3,128,128]{2,1,0:T(8,128)}, s32[]{:T(128)}) %tuple.29), condition=%wide.while_cond, body=%wide.while_body.sunk | while | flops 2 | bytes 132705 | solution.py:33
  676.7 2.9 bitcast_dynamic-update-slice_fusion.2
  680.3 2.9 bitcast_dynamic-update-slice_fusion.2
  683.8 2.8 bitcast_dynamic-update-slice_fusion.2
  686.6 30.6 %custom-call.26 = f32[3,128,128]{1,2,0:T(8,128)S(1)} custom-call(f32[3,128,128]{2,1,0:T(8,128)} %get-tuple-element.10), custom_call_target="InvertDiagBlocksLowerTriangular" | custom-call | tf_op jit(solution)/shard_map/triangular_solve | solution.py:33
  717.2 24.2 %all-reduce.8.cloned.1.call-done = f32[768,768]{0,1:T(8,128)} async-done(((f32[768,768]{0,1:T(8,128)}), f32[768,768]{0,1:T(8,128)}) %all-reduce.8.cloned.1.call-update) | async-done | bytes 2359312 | tf_op jit(solution)/shard_map/psum | solution.py:25
  741.4 2.7 fusion.2
  752.3 5.5 copy.34
  (48 shorter events, 19.9 us)
Async XLA Ops:
  7.2 340.3 %copy-start = (bf16[768,2048]{1,0:T(8,128)(2,1)S(1)}, bf16[768,2048]{1,0:T(8,128)(2,1)}, u32[]{:S(2)}) copy-start(bf16[768,2048]{1,0:T(8,128)(2,1)} %param.10) | copy-start | bytes 9437188
  27.8 172.6 %all-to-all-start = ((bf16[256,8,3696]{0,2,1:T(8,128)(2,1)}), bf16[256,8,3696]{0,2,1:T(8,128)(2,1)}, u32[]{:S(2)}, u32[]{:S(2)}) async-start(bf16[256,8,3696]{0,2,1:T(8,128)(2,1)} %bitcast.70), calls=%async_computation | async-start | bytes 30277632 | tf_op jit(solution)/shard_map/all_to_all | solution.py:11
  33.4 314.1 %all-reduce.6.cloned.1.call-start = ((), (), s32[]{:S(2)}) async-start(), calls=%async_computation.1 | async-start | bytes 6291456 | tf_op jit(solution)/shard_map/psum | solution.py:16
  247.3 20.1 %copy-start.4 = (bf16[3696,384]{1,0:T(8,128)(2,1)S(1)}, bf16[3696,384]{1,0:T(8,128)(2,1)}, u32[]{:S(2)}) copy-start(bf16[3696,384]{1,0:T(8,128)(2,1)} %param.8) | copy-start | bytes 8515588
  262.1 5.3 copy-start.1
  277.6 322.4 %all-reduce.10.cloned.1.call-start = ((), (), s32[]{:S(2)}) async-start(), calls=%async_computation.3 | async-start | bytes 13713408 | tf_op jit(solution)/shard_map/psum | solution.py:18
  358.0 383.4 %all-reduce.8.cloned.1.call-start = ((), (), s32[]{:S(2)}) async-start(), calls=%async_computation.2 | async-start | bytes 4718592 | tf_op jit(solution)/shard_map/psum | solution.py:25
  607.9 0.8 copy-start.3
  741.4 9.2 %copy-start.2 = (f32[2048,384]{1,0:T(8,128)S(1)}, f32[2048,384]{1,0:T(8,128)}, u32[]{:S(2)}) copy-start(f32[2048,384]{1,0:T(8,128)} %all-reduce.6.cloned.1.call-done) | copy-start | bytes 9437188
Sparse Core Ops, SparseCore 0:
  277.7 69.6 all-reduce.5
  358.1 241.8 all-reduce.9
  606.0 135.2 all-reduce.7
where the time goes:
time: 774 us; the launch traced here: 765 us
  waiting for transfers between devices  435 us (56%)
  other arithmetic  124 us (16%)
  local copies, waits for them, and re-layouts  96.5 us (12%)
  matrix products  86.7 us (11%)
  between operations  16.3 us (2%)
    psum x1, waiting for transfers between devices, local(): corange_sketch = lax.psum(corange_part, 'row')  208 us
    all_to_all x1, waiting for transfers between devices, local(): lax.all_to_all(adjusted_rows, 'col', split_axis=1, concat_axis=0, tiled=T...  148 us
    another operation x10, other arithmetic, local(): factor = jnp.linalg.cholesky(gram_matrix)  57.6 us
    psum x1, waiting for transfers between devices, local(): range_sketch = lax.psum(range_part, 'col')  55.5 us
    unnamed x14, local copies, waits for them, and re-layouts  52.9 us
    another operation x4, other arithmetic, local(): lax.linalg.triangular_solve(factor, halfway, left_side=True, lower=True,...  33.2 us
    convert_element_type x1, local copies, waits for them, and re-layouts, local(): adjusted_block.astype(jnp.float32) - base_weight.astype(jnp.float32)  30.1 us
    psum x1, waiting for transfers between devices, local(): core_sketch = lax.psum(partial_value, ('row', 'col'))  24.2 us
  transfers between devices with their start and end apart: 4, of which 4 were waited for; matrix products, arithmetic and copies ran while one was open for 24% of the time, Pallas kernels for 0%

commit v1 on v0

v1 whole, which is shorter than its diff:
```python
import jax
import jax.numpy as jnp
from jax import lax
from jax.experimental import pallas as pl
from jax.experimental.pallas import tpu as pltpu
from jax.sharding import PartitionSpec as P

BLOCK = 128


def invert_block(a):
    n = a.shape[0]
    lane = lax.broadcasted_iota(jnp.int32, (1, n), 1)
    sub = lax.broadcasted_iota(jnp.int32, (n, 1), 0)
    for j in range(n):
        inv = 1.0 / a[j : j + 1, j : j + 1]
        col = a[:, j : j + 1]
        row = jnp.where(lane == j, inv, a[j : j + 1, :] * inv)
        rest = jnp.where(lane == j, 0.0, a)
        a = jnp.where(sub == j, row, rest - col * row)
    return a


def solve_kernel(gram_ref, right_ref, out_ref, work):
    k_size = gram_ref.shape[0]
    width = right_ref.shape[1]
    work[:, :k_size] = gram_ref[...]
    work[:, k_size : k_size + width] = right_ref[...]

    def step(k, carry):
        at = pl.multiple_of(k * BLOCK, BLOCK)
        inverse = invert_block(work[pl.ds(at, BLOCK), pl.ds(at, BLOCK)])
        pivot = jnp.dot(inverse, work[pl.ds(at, BLOCK), :], precision=lax.Precision.HIGHEST,
                        preferred_element_type=jnp.float32)
        column = work[:, pl.ds(at, BLOCK)]
        work[...] -= jnp.dot(column, pivot, precision=lax.Precision.HIGHEST,
                             preferred_element_type=jnp.float32)
        work[pl.ds(at, BLOCK), :] = pivot
        return carry

    lax.fori_loop(0, k_size // BLOCK, step, 0)
    out_ref[...] = work[:, k_size : k_size + width]


def solve(gram, right_hand):
    k_size, width = right_hand.shape
    padded = -(-width // 128) * 128
    right_hand = jnp.pad(right_hand, ((0, 0), (0, padded - width)))
    solved = pl.pallas_call(
        solve_kernel,
        out_shape=jax.ShapeDtypeStruct((k_size, padded), jnp.float32),
        scratch_shapes=[pltpu.VMEM((k_size, k_size + padded), jnp.float32)],
        compiler_params=pltpu.CompilerParams(vmem_limit_bytes=16 * 1024 * 1024),
    )(gram, right_hand)
    return solved[:, :width]


def local(adjusted_rows, base_weight, range_test, corange_test, core_left, core_right):
    highest = lax.Precision.HIGHEST
    f32, bf16 = jnp.float32, jnp.bfloat16
    n_col = lax.axis_size("col")
    rows = adjusted_rows.shape[0]
    width = base_weight.shape[1]
    rank = corange_test.shape[0]
    side = core_left.shape[0]
    step = 128 if rows % 128 == 0 else rows
    left_tests = jnp.concatenate([core_left, corange_test], 0).reshape(side + rank, n_col, rows)
    base_blocks = base_weight.reshape(n_col, rows, width)
    range_parts, left_sum = [], None
    for at in range(0, rows, step):
        block = adjusted_rows[at : at + step].reshape(step, n_col, width).transpose(1, 0, 2)
        block = lax.all_to_all(block, "col", split_axis=0, concat_axis=0, tiled=True)
        difference = (
            block.astype(f32) - base_blocks[:, at : at + step].astype(f32)
        ).astype(bf16).reshape(n_col * step, width)
        tests = left_tests[:, :, at : at + step].reshape(side + rank, n_col * step)
        term = jnp.dot(tests, difference, preferred_element_type=f32)
        left_sum = term if left_sum is None else left_sum + term
        range_parts.append(
            jnp.dot(difference, range_test, preferred_element_type=f32).reshape(n_col, step, rank)
        )
    left_product, corange_part = left_sum[:side], left_sum[side:]
    high = lax.reduce_precision(left_product, 8, 7)
    low = (left_product - high).astype(bf16)
    pieces = jnp.concatenate([high.astype(bf16), low], 0)
    core_two = lax.dot_general(
        pieces, core_right, (((1,), (1,)), ((), ())), preferred_element_type=f32
    )
    projected_two = jnp.dot(pieces, range_test, preferred_element_type=f32)
    both = jnp.concatenate(
        [core_two[:side] + core_two[side:], projected_two[:side] + projected_two[side:]], 1
    )
    both = lax.psum(both, ("row", "col"))
    range_part = jnp.concatenate(range_parts, 1).reshape(n_col * rows, rank)
    both, range_part, corange_part = lax.optimization_barrier(
        (both, range_part, corange_part.astype(bf16))
    )
    range_sketch = lax.psum(range_part, "col")
    corange_sketch = lax.psum(corange_part, "row").astype(f32)
    share = side // n_col
    projected = both[:, side:]
    own_columns = lax.dynamic_slice_in_dim(both, lax.axis_index("col") * share, share, 1)
    gram = jnp.dot(projected.T, projected, precision=highest)
    right_hand = jnp.dot(projected.T, own_columns, precision=highest)
    return (range_sketch, corange_sketch, solve(gram, right_hand))


def solution(mesh):
    in_specs = (
        P(("row", "col"), None),
        P("row", "col"),
        P("col", None),
        P(None, "row"),
        P(None, "row"),
        P(None, "col"),
    )
    out_specs = (P("row", None), P(None, "col"), P(None, "col"))
    return jax.shard_map(local, mesh=mesh, in_specs=in_specs, out_specs=out_specs, check_vma=False)
```

time: 774 us -> 613 us (0.79)
  other arithmetic: 124 us -> 24.5 us
  waiting for transfers between devices: 435 us -> 341 us
  Pallas kernels: 0 us -> 36.8 us
    another operation x14 -> x0, other arithmetic: 90.9 us -> none  [the longest x10 57.6 us: local(): factor = jnp.linalg.cholesky(gram_matrix)]
    all_to_all x1 -> x2, waiting for transfers between devices: 148 us -> 82.3 us  [local(): lax.all_to_all(block, 'col', split_axis=0, concat_axis=0, tiled=True)]
    psum x2, waiting for transfers between devices: 232 us -> 190 us  [the longest x1 122 us: local(): both = lax.psum(both, ('row', 'col'))]
    pallas_call x0 -> x1, Pallas kernels: none -> 36.8 us  [solve(): pl.pallas_call(solve_kernel, out_shape=jax.ShapeDtypeStruct((k_size, padd...]
    convert_element_type x1 -> x0, local copies, waits for them, and re-layouts: 30.1 us -> none  [local(): adjusted_block.astype(jnp.float32) - base_weight.astype(jnp.float32)]
    slice x0 -> x3, local copies, waits for them, and re-layouts: none -> 25.9 us  [the longest x1 10.7 us: local(): adjusted_rows[at:at + step].reshape(step, n_col, width).transpose(1, 0, 2)]
    unnamed x14 -> x15, local copies, waits for them, and re-layouts: 52.9 us -> 75.5 us
    convert_element_type x2, other arithmetic: 31.6 us -> 14.9 us  [the longest x1 10.3 us: local(): pieces = jnp.concatenate([high.astype(bf16), low], 0)]
  transfers between devices with their start and end apart: 4 -> 5, of which waited for: 4 -> 5; matrix products, arithmetic and copies ran while one was open for 24% -> 19% of each run, Pallas kernels for 0% -> 6%
where the time goes in v1:
time: 613 us; the launch traced here: 611 us
  waiting for transfers between devices  341 us (56%)
  local copies, waits for them, and re-layouts  101 us (16%)
  matrix products  83.5 us (14%)
  Pallas kernels  36.8 us (6%)
  other arithmetic  24.5 us (4%)
  between operations  13.8 us (2%)
  starting transfers between devices  10.2 us (2%)
    psum x1, waiting for transfers between devices, local(): both = lax.psum(both, ('row', 'col'))  122 us
    all_to_all x2, waiting for transfers between devices, local(): lax.all_to_all(block, 'col', split_axis=0, concat_axis=0, tiled=True)  82.3 us
    unnamed x15, local copies, waits for them, and re-layouts  75.5 us
    psum x1, waiting for transfers between devices, local(): corange_sketch = lax.psum(corange_part, 'row').astype(f32)  68.5 us
    psum x1, waiting for transfers between devices, local(): range_sketch = lax.psum(range_part, 'col')  67.7 us
    dot_general x2, matrix products, local(): term = jnp.dot(tests, difference, preferred_element_type=f32)  37 us
    pallas_call x1, Pallas kernels, solve(): pl.pallas_call(solve_kernel, out_shape=jax.ShapeDtypeStruct((k_size, padd...  36.8 us
    dot_general x1, matrix products, local(): lax.dot_general(pieces, core_right, (((1,), (1,)), ((), ())), preferred_e...  15.8 us
  transfers between devices with their start and end apart: 5, of which 5 were waited for; matrix products, arithmetic and copies ran while one was open for 19% of the time, Pallas kernels for 6%

profile of v1, /device:TPU:0, one launch (start us, length us, event | category | flops | bytes accessed | tf_op | source)
XLA Modules:
  0.0 611.3 jit_solution(15017323912392707735)
XLA Ops:
  7.2 10.7 %fusion.19 = (bf16[128,29568]{1,0:T(8,128)(2,1)}, bf16[128,29568]{1,0:T(8,128)(2,1)}) fusion(bf16[256,29568]{1,0:T(8,128)(2,1)} %param.6), kind=kLoop, calls=%fused_computation.32 | loop fusion | bytes 30277632 | tf_op jit(solution)/shard_map/slice | solution.py:71
  17.9 10.5 %copy.62 = bf16[128,29568]{0,1:T(8,128)(2,1)} copy(bf16[128,29568]{1,0:T(8,128)(2,1)} %get-tuple-element.29) | data formatting | bytes 15138816
  28.4 5.2 all-to-all-start
  33.5 10.5 %copy.65 = bf16[128,29568]{0,1:T(8,128)(2,1)} copy(bf16[128,29568]{1,0:T(8,128)(2,1)} %get-tuple-element.28) | data formatting | bytes 15138816
  44.0 75.2 %all-to-all-done = bf16[8,128,3696]{1,2,0:T(8,128)(2,1)} async-done(((bf16[8,128,3696]{1,2,0:T(8,128)(2,1)}), bf16[8,128,3696]{1,2,0:T(8,128)(2,1)}, u32[]{:S(2)}, u32[]{:S(2)}) %all-to-all-start) | async-done | bytes 7569440 | tf_op jit(solution)/shard_map/all_to_all | solution.py:72
  119.2 4.9 all-to-all-start.1
  124.2 2.6 copy.50
  126.7 4.6 copy.49
  131.4 19.0 %copy.53 = bf16[2048,3696]{1,0:T(8,128)(2,1)} copy(bf16[2048,3696]{0,1:T(8,128)(2,1)} %param.7) | data formatting | bytes 30277632 | tf_op args[1]
  150.4 10.6 %fusion.18 = (bf16[8,128,3696]{2,1,0:T(8,128)(2,1)}, bf16[8,128,3696]{2,1,0:T(8,128)(2,1)}) fusion(bf16[8,256,3696]{2,1,0:T(8,128)(2,1)} %bitcast.24), kind=kLoop, calls=%fused_computation.31 | loop fusion | bytes 30277632 | tf_op jit(solution)/shard_map/slice | solution.py:74
  161.0 10.1 %copy.66 = bf16[8,128,3696]{1,2,0:T(8,128)(2,1)} copy(bf16[8,128,3696]{2,1,0:T(8,128)(2,1)} %get-tuple-element.26) | data formatting | bytes 15138816
  171.1 10.3 %copy.63 = bf16[8,128,3696]{1,2,0:T(8,128)(2,1)} copy(bf16[8,128,3696]{2,1,0:T(8,128)(2,1)} %get-tuple-element.27) | data formatting | bytes 15138816
  181.4 2.9 pad_maximum_fusion.3
  184.3 2.4 copy-done.2
  187.6 14.6 %convolution_bitcast_fusion.1 = f32[1152,3696]{0,1:T(8,128)} fusion(bf16[8,128,3696]{1,2,0:T(8,128)(2,1)S(1)} %copy-done.1, bf16[8,128,3696]{1,2,0:T(8,128)(2,1)} %all-to-all-done, bf16[1152,8,256]{0,2,1:T(8,128)(2,1)S(1)} %bitcast.28), kind=kOutput, calls=%fused_computation.2 | convolution fusion | flops 8735096832 | bytes 34529280 | tf_op jit(solution)/shard_map/dot_general | solution.py:77
  202.3 7.1 %all-to-all-done.1 = bf16[8,128,3696]{1,2,0:T(8,128)(2,1)} async-done(((bf16[8,128,3696]{1,2,0:T(8,128)(2,1)}), bf16[8,128,3696]{1,2,0:T(8,128)(2,1)}, u32[]{:S(2)}, u32[]{:S(2)}) %all-to-all-start.1) | async-done | bytes 7569440 | tf_op jit(solution)/shard_map/all_to_all | solution.py:72
  209.4 22.4 %fusion = f32[1152,3696]{0,1:T(8,128)} fusion(f32[1152,3696]{0,1:T(8,128)} %convolution_bitcast_fusion.1, bf16[8,128,3696]{1,2,0:T(8,128)(2,1)} %copy.66, bf16[8,128,3696]{1,2,0:T(8,128)(2,1)} %all-to-all-done.1, bf16[1152,8,256]{0,2,1:T(8,128)(2,1)} %bitcast.29), kind=kOutput, calls=%fused_computation.1 | convolution fusion | flops 8739354624 | bytes 51560448 | tf_op jit(solution)/shard_map/dot_general | solution.py:77
  231.8 4.6 slice.83
  236.4 10.3 %reduce-precision_convert_fusion = (bf16[768,3696]{0,1:T(8,128)(2,1)}, bf16[768,3696]{0,1:T(8,128)(2,1)}) fusion(f32[1152,3696]{0,1:T(8,128)} %fusion), kind=kLoop, calls=%fused_computation.4 | loop fusion | flops 11354112 | bytes 22708224 | tf_op jit(solution)/shard_map/convert_element_type | solution.py:85
  246.7 9.1 %fusion.2 = f32[1536,384]{0,1:T(8,128)S(1)} fusion(bf16[3696,384]{1,0:T(8,128)(2,1)S(1)} %copy-done, bf16[768,3696]{0,1:T(8,128)(2,1)} %get-tuple-element.25, bf16[768,3696]{0,1:T(8,128)(2,1)} %get-tuple-element.24), kind=kOutput, calls=%fused_computation.9 | convolution fusion | flops 4382687232 | bytes 16551936 | tf_op jit(solution)/shard_map/dot_general | solution.py:89
  255.8 15.8 %fusion.3 = f32[1536,768]{0,1:T(8,128)} fusion(bf16[768,3696]{0,1:T(8,128)(2,1)} %param.11, bf16[768,3696]{0,1:T(8,128)(2,1)} %get-tuple-element.25, bf16[768,3696]{0,1:T(8,128)(2,1)} %get-tuple-element.24), kind=kOutput, calls=%fused_computation.10 | convolution fusion | flops 8742666240 | bytes 21749760 | tf_op jit(solution)/shard_map/dot_general | solution.py:86
  271.6 2.7 slice_add_fusion
  276.5 7.7 %fusion.5 = f32[8,128,384]{2,1,0:T(8,128)S(1)} fusion(bf16[8,128,3696]{1,2,0:T(8,128)(2,1)} %copy.66, bf16[8,128,3696]{1,2,0:T(8,128)(2,1)} %all-to-all-done.1, bf16[3696,384]{1,0:T(8,128)(2,1)S(1)} %copy-done), kind=kOutput, calls=%fused_computation.16 | convolution fusion | flops 2921791488 | bytes 19550208 | tf_op jit(solution)/shard_map/dot_general | solution.py:80
  284.2 7.8 %fusion.4 = f32[8,128,384]{2,1,0:T(8,128)S(1)} fusion(bf16[8,128,3696]{1,2,0:T(8,128)(2,1)} %copy.63, bf16[8,128,3696]{1,2,0:T(8,128)(2,1)} %all-to-all-done, bf16[3696,384]{1,0:T(8,128)(2,1)S(1)} %copy-done), kind=kOutput, calls=%fused_computation.15 | convolution fusion | flops 2921791488 | bytes 19550208 | tf_op jit(solution)/shard_map/dot_general | solution.py:80
  293.9 121.7 %all-reduce.5.cloned.1.call-done = f32[768,1152]{0,1:T(8,128)} async-done(((f32[768,1152]{0,1:T(8,128)}), f32[768,1152]{0,1:T(8,128)}) %all-reduce.5.cloned.1.call-update) | async-done | bytes 3538960 | tf_op jit(solution)/shard_map/psum | solution.py:93
  416.4 2.4 fusion.10
  418.8 3.7 fusion.12.gram_ref
  422.5 36.8 %shard_map.85 = f32[384,128]{1,0:T(8,128)S(1)} custom-call(f32[384,384]{1,0:T(8,128)S(1)} %fusion.12.gram_ref, f32[384,128]{1,0:T(8,128)S(1)} %pad.4.right_ref), custom_call_target="tpu_custom_call" | custom-call | tf_op jit(solution)/shard_map/pallas_call | solution.py:49
  460.1 68.5 %all-reduce.9.cloned.1.call-done = bf16[384,3696]{0,1:T(8,128)(2,1)} async-done(((bf16[384,3696]{0,1:T(8,128)(2,1)}), bf16[384,3696]{0,1:T(8,128)(2,1)}) %all-reduce.9.cloned.1.call-update) | async-done | bytes 2838544 | tf_op jit(solution)/shard_map/psum | solution.py:99
  528.6 4.7 convert_element_type.38
  533.3 67.7 %all-reduce.7.cloned.1.call-done = f32[2048,384]{1,0:T(8,128)} async-done(((f32[2048,384]{1,0:T(8,128)}), f32[2048,384]{1,0:T(8,128)}) %all-reduce.7.cloned.1.call-update) | async-done | bytes 3145744 | tf_op jit(solution)/shard_map/psum | solution.py:98
  601.0 3.8 copy.70
  (16 shorter events, 6.7 us)
Async XLA Ops:
  7.2 239.5 %copy-start = (bf16[3696,384]{1,0:T(8,128)(2,1)S(1)}, bf16[3696,384]{1,0:T(8,128)(2,1)}, u32[]{:S(2)}) copy-start(bf16[3696,384]{1,0:T(8,128)(2,1)} %param.8) | copy-start | bytes 8515588
  28.4 90.8 %all-to-all-start = ((bf16[8,128,3696]{1,2,0:T(8,128)(2,1)}), bf16[8,128,3696]{1,2,0:T(8,128)(2,1)}, u32[]{:S(2)}, u32[]{:S(2)}) async-start(bf16[8,128,3696]{1,2,0:T(8,128)(2,1)} %bitcast.26), calls=%async_computation | async-start | bytes 15138816 | tf_op jit(solution)/shard_map/all_to_all | solution.py:72
  119.2 90.2 %all-to-all-start.1 = ((bf16[8,128,3696]{1,2,0:T(8,128)(2,1)}), bf16[8,128,3696]{1,2,0:T(8,128)(2,1)}, u32[]{:S(2)}, u32[]{:S(2)}) async-start(bf16[8,128,3696]{1,2,0:T(8,128)(2,1)} %bitcast.25), calls=%async_computation.1 | async-start | bytes 15138816 | tf_op jit(solution)/shard_map/all_to_all | solution.py:72
  124.1 291.5 %all-reduce.5.cloned.1.call-start = ((), (), s32[]{:S(2)}) async-start(), calls=%async_computation.2 | async-start | bytes 7077888 | tf_op jit(solution)/shard_map/psum | solution.py:93
  181.4 6.2 %copy-start.1 = (bf16[8,128,3696]{1,2,0:T(8,128)(2,1)S(1)}, bf16[8,128,3696]{1,2,0:T(8,128)(2,1)}, u32[]{:S(2)}) copy-start(bf16[8,128,3696]{1,2,0:T(8,128)(2,1)} %copy.63) | copy-start | bytes 22708228
  184.3 2.4 copy-start.2
  276.5 252.2 %all-reduce.9.cloned.1.call-start = ((), (), s32[]{:S(2)}) async-start(), calls=%async_computation.4 | async-start | bytes 5677056 | tf_op jit(solution)/shard_map/psum | solution.py:99
  415.7 185.3 %all-reduce.7.cloned.1.call-start = ((), (), s32[]{:S(2)}) async-start(), calls=%async_computation.3 | async-start | bytes 6291456 | tf_op jit(solution)/shard_map/psum | solution.py:98
Sparse Core Ops, SparseCore 0:
  276.6 139.0 all-reduce.4
  418.2 110.4 all-reduce.8
  532.5 68.4 all-reduce.6

commit v2 on v1

--- a/solution.py
+++ b/solution.py
@@ -80,28 +80,33 @@
             jnp.dot(difference, range_test, preferred_element_type=f32).reshape(n_col, step, rank)
         )
     left_product, corange_part = left_sum[:side], left_sum[side:]
+    corange_sketch = lax.psum(corange_part.astype(bf16), "row").astype(f32)
     high = lax.reduce_precision(left_product, 8, 7)
     low = (left_product - high).astype(bf16)
     pieces = jnp.concatenate([high.astype(bf16), low], 0)
     core_two = lax.dot_general(
-        pieces, core_right, (((1,), (1,)), ((), ())), preferred_element_type=f32
+        core_right, pieces, (((1,), (1,)), ((), ())), preferred_element_type=f32
     )
-    projected_two = jnp.dot(pieces, range_test, preferred_element_type=f32)
-    both = jnp.concatenate(
-        [core_two[:side] + core_two[side:], projected_two[:side] + projected_two[side:]], 1
+    projected_two = lax.dot_general(
+        range_test, pieces, (((0,), (1,)), ((), ())), preferred_element_type=f32
     )
-    both = lax.psum(both, ("row", "col"))
-    range_part = jnp.concatenate(range_parts, 1).reshape(n_col * rows, rank)
-    both, range_part, corange_part = lax.optimization_barrier(
-        (both, range_part, corange_part.astype(bf16))
+    share, narrow = side // n_col, rank // n_col
+    core_term = (core_two[:, :side] + core_two[:, side:]).reshape(n_col, share, side)
+    projected_term = (projected_two[:, :side] + projected_two[:, side:]).reshape(
+        n_col, narrow, side
     )
-    range_sketch = lax.psum(range_part, "col")
-    corange_sketch = lax.psum(corange_part, "row").astype(f32)
-    share = side // n_col
-    projected = both[:, side:]
-    own_columns = lax.dynamic_slice_in_dim(both, lax.axis_index("col") * share, share, 1)
-    gram = jnp.dot(projected.T, projected, precision=highest)
-    right_hand = jnp.dot(projected.T, own_columns, precision=highest)
+    both = jnp.concatenate([core_term, projected_term], 1)
+    both = lax.all_to_all(both, "col", split_axis=0, concat_axis=0, tiled=True).sum(0)
+    range_part = jnp.concatenate(range_parts, 1)
+    both, range_part = lax.optimization_barrier((both, range_part.astype(bf16)))
+    both = lax.psum(both, "row")
+    projected = lax.all_gather(both[share:], "col", axis=0, tiled=True)
+    range_own = lax.all_to_all(range_part, "col", split_axis=0, concat_axis=0, tiled=True)
+    range_own = range_own.astype(f32).sum(0).astype(bf16)
+    projected, range_own = lax.optimization_barrier((projected, range_own))
+    range_sketch = lax.all_gather(range_own, "col", axis=0, tiled=True).astype(f32)
+    gram = jnp.dot(projected, projected.T, precision=highest)
+    right_hand = jnp.dot(projected, both[:share].T, precision=highest)
     return (range_sketch, corange_sketch, solve(gram, right_hand))
 
 

time: 613 us -> 574 us (0.936); the launches traced: 611 us -> 565 us
  waiting for transfers between devices: 341 us -> 256 us
  blocking collectives: 0 us -> 29 us
  other arithmetic: 24.5 us -> 32.8 us
    psum x3 -> x2, waiting for transfers between devices: 258 us -> 150 us  [the longest x1 113 us: local(): corange_sketch = lax.psum(corange_part.astype(bf16), 'row').astype(f32)]
    all_to_all x0 -> x1, blocking collectives: none -> 29 us  [local(): lax.all_to_all(range_part, 'col', split_axis=0, concat_axis=0, tiled=True)]
    all_to_all x0 -> x1, waiting for transfers between devices: none -> 23.9 us  [local(): lax.all_to_all(both, 'col', split_axis=0, concat_axis=0, tiled=True).sum(0)]
    unnamed x15 -> x18, local copies, waits for them, and re-layouts: 75.5 us -> 71.8 us
  transfers between devices with their start and end apart: 5 -> 7, of which waited for: 5 -> 5; matrix products, arithmetic and copies ran while one was open for 19% -> 21% of each run, Pallas kernels for 6% -> 6%
where the time goes in v2:
time: 574 us; the launch traced here: 565 us
  waiting for transfers between devices  256 us (45%)
  local copies, waits for them, and re-layouts  99.2 us (17%)
  matrix products  82.2 us (14%)
  Pallas kernels  36.5 us (6%)
  other arithmetic  32.8 us (6%)
  blocking collectives  29 us (5%)
  starting transfers between devices  15 us (3%)
  between operations  14.3 us (2%)
    psum x1, waiting for transfers between devices, local(): corange_sketch = lax.psum(corange_part.astype(bf16), 'row').astype(f32)  113 us
    all_to_all x2, waiting for transfers between devices, local(): lax.all_to_all(block, 'col', split_axis=0, concat_axis=0, tiled=True)  82.1 us
    unnamed x18, local copies, waits for them, and re-layouts  71.8 us
    psum x1, waiting for transfers between devices, local(): both = lax.psum(both, 'row')  37.7 us
    dot_general x2, matrix products, local(): term = jnp.dot(tests, difference, preferred_element_type=f32)  37.4 us
    pallas_call x1, Pallas kernels, solve(): pl.pallas_call(solve_kernel, out_shape=jax.ShapeDtypeStruct((k_size, padd...  36.5 us
    all_to_all x1, blocking collectives, local(): lax.all_to_all(range_part, 'col', split_axis=0, concat_axis=0, tiled=True)  29 us
    all_to_all x1, waiting for transfers between devices, local(): lax.all_to_all(both, 'col', split_axis=0, concat_axis=0, tiled=True).sum(0)  23.9 us
  transfers between devices with their start and end apart: 7, of which 5 were waited for; matrix products, arithmetic and copies ran while one was open for 21% of the time, Pallas kernels for 6%

profile of v2, /device:TPU:0, one launch (start us, length us, event | category | flops | bytes accessed | tf_op | source)
XLA Modules:
  0.0 565.5 jit_solution(4154063325629252860)
XLA Ops:
  7.2 10.7 %fusion.23 = (bf16[128,29568]{1,0:T(8,128)(2,1)}, bf16[128,29568]{1,0:T(8,128)(2,1)}) fusion(bf16[256,29568]{1,0:T(8,128)(2,1)} %param.6), kind=kLoop, calls=%fused_computation.32 | loop fusion | bytes 30277632 | tf_op jit(solution)/shard_map/slice | solution.py:71
  17.9 10.5 %copy.62 = bf16[128,29568]{0,1:T(8,128)(2,1)} copy(bf16[128,29568]{1,0:T(8,128)(2,1)} %get-tuple-element.31) | data formatting | bytes 15138816
  28.3 5.2 all-to-all-start
  33.5 10.5 %copy.65 = bf16[128,29568]{0,1:T(8,128)(2,1)} copy(bf16[128,29568]{1,0:T(8,128)(2,1)} %get-tuple-element.30) | data formatting | bytes 15138816
  44.0 75.2 %all-to-all-done = bf16[8,128,3696]{1,2,0:T(8,128)(2,1)} async-done(((bf16[8,128,3696]{1,2,0:T(8,128)(2,1)}), bf16[8,128,3696]{1,2,0:T(8,128)(2,1)}, u32[]{:S(2)}, u32[]{:S(2)}) %all-to-all-start) | async-done | bytes 7569440 | tf_op jit(solution)/shard_map/all_to_all | solution.py:72
  119.1 4.9 all-to-all-start.1
  124.1 2.6 copy.50
  126.7 4.6 copy.49
  131.3 19.0 %copy.53 = bf16[2048,3696]{1,0:T(8,128)(2,1)} copy(bf16[2048,3696]{0,1:T(8,128)(2,1)} %param.7) | data formatting | bytes 30277632 | tf_op args[1]
  150.3 10.6 %fusion.22 = (bf16[8,128,3696]{2,1,0:T(8,128)(2,1)}, bf16[8,128,3696]{2,1,0:T(8,128)(2,1)}) fusion(bf16[8,256,3696]{2,1,0:T(8,128)(2,1)} %bitcast.36), kind=kLoop, calls=%fused_computation.31 | loop fusion | bytes 30277632 | tf_op jit(solution)/shard_map/slice | solution.py:74
  160.9 10.2 %copy.66 = bf16[8,128,3696]{1,2,0:T(8,128)(2,1)} copy(bf16[8,128,3696]{2,1,0:T(8,128)(2,1)} %get-tuple-element.28) | data formatting | bytes 15138816
  171.1 10.3 %copy.63 = bf16[8,128,3696]{1,2,0:T(8,128)(2,1)} copy(bf16[8,128,3696]{2,1,0:T(8,128)(2,1)} %get-tuple-element.29) | data formatting | bytes 15138816
  181.4 2.9 pad_maximum_fusion.3
  187.6 14.7 %convolution_bitcast_fusion.1 = f32[1152,3696]{0,1:T(8,128)} fusion(bf16[8,128,3696]{1,2,0:T(8,128)(2,1)S(1)} %copy-done.2, bf16[8,128,3696]{1,2,0:T(8,128)(2,1)} %all-to-all-done, bf16[1152,8,256]{0,2,1:T(8,128)(2,1)S(1)} %bitcast.41), kind=kOutput, calls=%fused_computation.2 | convolution fusion | flops 8735096832 | bytes 34529280 | tf_op jit(solution)/shard_map/dot_general | solution.py:77
  202.4 7.0 %all-to-all-done.1 = bf16[8,128,3696]{1,2,0:T(8,128)(2,1)} async-done(((bf16[8,128,3696]{1,2,0:T(8,128)(2,1)}), bf16[8,128,3696]{1,2,0:T(8,128)(2,1)}, u32[]{:S(2)}, u32[]{:S(2)}) %all-to-all-start.1) | async-done | bytes 7569440 | tf_op jit(solution)/shard_map/all_to_all | solution.py:72
  209.4 22.6 %fusion = f32[1152,3696]{0,1:T(8,128)} fusion(f32[1152,3696]{0,1:T(8,128)} %convolution_bitcast_fusion.1, bf16[8,128,3696]{1,2,0:T(8,128)(2,1)} %copy.66, bf16[8,128,3696]{1,2,0:T(8,128)(2,1)} %all-to-all-done.1, bf16[1152,8,256]{0,2,1:T(8,128)(2,1)} %bitcast.42), kind=kOutput, calls=%fused_computation.1 | convolution fusion | flops 8739354624 | bytes 51560448 | tf_op jit(solution)/shard_map/dot_general | solution.py:77
  232.0 10.3 %reduce-precision_convert_fusion = (bf16[768,3696]{0,1:T(8,128)(2,1)}, bf16[768,3696]{0,1:T(8,128)(2,1)}) fusion(f32[1152,3696]{0,1:T(8,128)} %fusion), kind=kLoop, calls=%fused_computation.4 | loop fusion | flops 11354112 | bytes 22708224 | tf_op jit(solution)/shard_map/convert_element_type | solution.py:86
  242.3 9.1 %fusion.5 = f32[384,1536]{1,0:T(8,128)S(1)} fusion(bf16[3696,384]{1,0:T(8,128)(2,1)S(1)} %copy-done, bf16[768,3696]{0,1:T(8,128)(2,1)} %get-tuple-element.27, bf16[768,3696]{0,1:T(8,128)(2,1)} %get-tuple-element.26), kind=kOutput, calls=%fused_computation.15 | convolution fusion | flops 4382687232 | bytes 16551936 | tf_op jit(solution)/shard_map/dot_general | solution.py:90
  251.4 15.7 %fusion.4 = f32[768,1536]{1,0:T(8,128)} fusion(bf16[768,3696]{0,1:T(8,128)(2,1)} %param.11, bf16[768,3696]{0,1:T(8,128)(2,1)} %get-tuple-element.27, bf16[768,3696]{0,1:T(8,128)(2,1)} %get-tuple-element.26), kind=kOutput, calls=%fused_computation.13 | convolution fusion | flops 8742666240 | bytes 21749760 | tf_op jit(solution)/shard_map/dot_general | solution.py:87
  267.1 2.7 slice_add_fusion
  272.1 4.7 all-to-all-start.2
  276.8 8.4 %fusion.12 = bf16[8,128,384]{2,1,0:T(8,128)(2,1)S(1)} fusion(bf16[3696,384]{1,0:T(8,128)(2,1)S(1)} %copy-done, bf16[8,128,3696]{1,2,0:T(8,128)(2,1)} %copy.66, bf16[8,128,3696]{1,2,0:T(8,128)(2,1)} %all-to-all-done.1), kind=kOutput, calls=%fused_computation.24 | convolution fusion | flops 2922184704 | bytes 18763776 | tf_op jit(solution)/shard_map/dot_general | solution.py:80
  285.3 8.4 %fusion.15 = bf16[8,128,384]{2,1,0:T(8,128)(2,1)S(1)} fusion(bf16[3696,384]{1,0:T(8,128)(2,1)S(1)} %copy-done, bf16[8,128,3696]{1,2,0:T(8,128)(2,1)} %copy.63, bf16[8,128,3696]{1,2,0:T(8,128)(2,1)} %all-to-all-done), kind=kOutput, calls=%fused_computation.25 | convolution fusion | flops 2922184704 | bytes 18763776 | tf_op jit(solution)/shard_map/dot_general | solution.py:80
  295.0 23.9 %all-to-all-done.2 = f32[8,144,768]{2,1,0:T(8,128)} async-done(((f32[8,144,768]{2,1,0:T(8,128)}), f32[8,144,768]{2,1,0:T(8,128)}, u32[]{:S(2)}, u32[]{:S(2)}) %all-to-all-start.2) | async-done | bytes 3538976 | tf_op jit(solution)/shard_map/all_to_all | solution.py:99
  318.9 3.0 reduce_sum.21
  322.0 37.7 %all-reduce.4.cloned.1.call-done = f32[144,768]{1,0:T(8,128)} async-done(((f32[144,768]{1,0:T(8,128)}), f32[144,768]{1,0:T(8,128)}) %all-reduce.4.cloned.1.call-update) | async-done | bytes 442384 | tf_op jit(solution)/shard_map/psum | solution.py:102
  361.3 4.5 slice.87
  365.8 29.0 %all_to_all.20 = bf16[8,256,384]{2,1,0:T(8,128)(2,1)} all-to-all(bf16[8,256,384]{2,1,0:T(8,128)(2,1)} %pad_maximum_fusion.9), channel_id=1, replica_groups=mesh['row'=4,'col'=8] {'col'}, dimensions={0} | all-to-all | bytes 3145728 | tf_op jit(solution)/shard_map/all_to_all | solution.py:104
  397.3 112.6 %all-reduce.6.cloned.1.call-done = bf16[384,3696]{0,1:T(8,128)(2,1)} async-done(((bf16[384,3696]{0,1:T(8,128)(2,1)}), bf16[384,3696]{0,1:T(8,128)(2,1)}) %all-reduce.6.cloned.1.call-update) | async-done | bytes 2838544 | tf_op jit(solution)/shard_map/psum | solution.py:83
  509.9 4.8 convert_element_type.45
  517.9 36.5 %shard_map.85 = f32[384,128]{1,0:T(8,128)S(1)} custom-call(f32[384,384]{1,0:T(8,128)S(1)} %fusion.24.gram_ref, f32[384,128]{1,0:T(8,128)S(1)} %pad.4.right_ref), custom_call_target="tpu_custom_call" | custom-call | tf_op jit(solution)/shard_map/pallas_call | solution.py:49
  555.2 3.3 convert_element_type.44
  (29 shorter events, 15.1 us)
Async XLA Ops:
  7.2 235.1 %copy-start = (bf16[3696,384]{1,0:T(8,128)(2,1)S(1)}, bf16[3696,384]{1,0:T(8,128)(2,1)}, u32[]{:S(2)}) copy-start(bf16[3696,384]{1,0:T(8,128)(2,1)} %param.8) | copy-start | bytes 8515588
  28.3 90.8 %all-to-all-start = ((bf16[8,128,3696]{1,2,0:T(8,128)(2,1)}), bf16[8,128,3696]{1,2,0:T(8,128)(2,1)}, u32[]{:S(2)}, u32[]{:S(2)}) async-start(bf16[8,128,3696]{1,2,0:T(8,128)(2,1)} %bitcast.38), calls=%async_computation | async-start | bytes 15138816 | tf_op jit(solution)/shard_map/all_to_all | solution.py:72
  119.1 90.2 %all-to-all-start.1 = ((bf16[8,128,3696]{1,2,0:T(8,128)(2,1)}), bf16[8,128,3696]{1,2,0:T(8,128)(2,1)}, u32[]{:S(2)}, u32[]{:S(2)}) async-start(bf16[8,128,3696]{1,2,0:T(8,128)(2,1)} %bitcast.37), calls=%async_computation.1 | async-start | bytes 15138816 | tf_op jit(solution)/shard_map/all_to_all | solution.py:72
  181.4 6.2 %copy-start.2 = (bf16[8,128,3696]{1,2,0:T(8,128)(2,1)S(1)}, bf16[8,128,3696]{1,2,0:T(8,128)(2,1)}, u32[]{:S(2)}) copy-start(bf16[8,128,3696]{1,2,0:T(8,128)(2,1)} %copy.63) | copy-start | bytes 22708228
  184.3 2.4 copy-start.3
  272.1 46.8 %all-to-all-start.2 = ((f32[8,144,768]{2,1,0:T(8,128)}), f32[8,144,768]{2,1,0:T(8,128)}, u32[]{:S(2)}, u32[]{:S(2)}) async-start(f32[8,144,768]{2,1,0:T(8,128)} %pad_maximum_fusion.6), calls=%async_computation.2 | async-start | bytes 7077888 | tf_op jit(solution)/shard_map/all_to_all | solution.py:99
  276.8 82.9 %all-reduce.4.cloned.1.call-start = ((), (), s32[]{:S(2)}) async-start(), calls=%async_computation.4 | async-start | bytes 884736 | tf_op jit(solution)/shard_map/psum | solution.py:102
  321.9 75.4 %all-gather.3.cloned.1.call-start = ((), (), s32[]{:S(2)}) async-start(), calls=%async_computation.5 | async-start | bytes 1327104 | tf_op jit(solution)/shard_map/all_gather | solution.py:103
  361.2 148.7 %all-reduce.6.cloned.1.call-start = ((), (), s32[]{:S(2)}) async-start(), calls=%async_computation.7 | async-start | bytes 5677056 | tf_op jit(solution)/shard_map/psum | solution.py:83
  365.8 189.4 %all-gather.5.cloned.1.call-start = ((), (), s32[]{:S(2)}) async-start(), calls=%async_computation.6 | async-start | bytes 1769472 | tf_op jit(solution)/shard_map/all_gather | solution.py:107
  394.9 119.8 %copy-start.4 = (f32[144,768]{1,0:T(8,128)S(1)}, f32[144,768]{1,0:T(8,128)}, u32[]{:S(2)}) copy-start(f32[144,768]{1,0:T(8,128)} %all-reduce.4.cloned.1.call-done) | copy-start | bytes 1327108
  509.9 4.8 copy-start.1
Sparse Core Ops, SparseCore 0:
  322.0 37.5 all-reduce.3
  362.3 31.9 all-gather.2
  397.3 112.5 all-reduce.5
  511.7 29.0 all-gather.4

commit v3 on v2

--- a/solution.py
+++ b/solution.py
@@ -80,7 +80,6 @@
             jnp.dot(difference, range_test, preferred_element_type=f32).reshape(n_col, step, rank)
         )
     left_product, corange_part = left_sum[:side], left_sum[side:]
-    corange_sketch = lax.psum(corange_part.astype(bf16), "row").astype(f32)
     high = lax.reduce_precision(left_product, 8, 7)
     low = (left_product - high).astype(bf16)
     pieces = jnp.concatenate([high.astype(bf16), low], 0)
@@ -101,6 +100,8 @@
     both, range_part = lax.optimization_barrier((both, range_part.astype(bf16)))
     both = lax.psum(both, "row")
     projected = lax.all_gather(both[share:], "col", axis=0, tiled=True)
+    projected, corange_part = lax.optimization_barrier((projected, corange_part.astype(bf16)))
+    corange_sketch = lax.psum(corange_part, "row").astype(f32)
     range_own = lax.all_to_all(range_part, "col", split_axis=0, concat_axis=0, tiled=True)
     range_own = range_own.astype(f32).sum(0).astype(bf16)
     projected, range_own = lax.optimization_barrier((projected, range_own))

time: 574 us -> 557 us (0.970)
  blocking collectives: 29 us -> 0 us
    all_to_all x1 -> x0, blocking collectives: 29 us -> none  [local(): lax.all_to_all(range_part, 'col', split_axis=0, concat_axis=0, tiled=True)]
    all_to_all x0 -> x1, waiting for transfers between devices: none -> 18.8 us  [local(): lax.all_to_all(range_part, 'col', split_axis=0, concat_axis=0, tiled=True)]
    psum x1, waiting for transfers between devices: 113 us -> 96.5 us  [local(): corange_sketch = lax.psum(corange_part, 'row').astype(f32)]
    unnamed x18 -> x16, local copies, waits for them, and re-layouts: 71.8 us -> 71.6 us
  transfers between devices with their start and end apart: 7 -> 8, of which waited for: 5 -> 7; matrix products, arithmetic and copies ran while one was open for 21% -> 22% of each run, Pallas kernels for 6% -> 7%
where the time goes in v3:
time: 557 us; the launch traced here: 548 us
  waiting for transfers between devices  261 us (47%)
  local copies, waits for them, and re-layouts  99 us (18%)
  matrix products  85.1 us (15%)
  Pallas kernels  36.5 us (7%)
  other arithmetic  32.6 us (6%)
  starting transfers between devices  19.6 us (4%)
  between operations  14.3 us (3%)
    psum x1, waiting for transfers between devices, local(): corange_sketch = lax.psum(corange_part, 'row').astype(f32)  96.5 us
    all_to_all x2, waiting for transfers between devices, local(): lax.all_to_all(block, 'col', split_axis=0, concat_axis=0, tiled=True)  82.3 us
    unnamed x16, local copies, waits for them, and re-layouts  71.6 us
    psum x1, waiting for transfers between devices, local(): both = lax.psum(both, 'row')  37.7 us
    dot_general x2, matrix products, local(): term = jnp.dot(tests, difference, preferred_element_type=f32)  37.3 us
    pallas_call x1, Pallas kernels, solve(): pl.pallas_call(solve_kernel, out_shape=jax.ShapeDtypeStruct((k_size, padd...  36.5 us
    all_to_all x1, waiting for transfers between devices, local(): lax.all_to_all(both, 'col', split_axis=0, concat_axis=0, tiled=True).sum(0)  23.9 us
    all_to_all x1, waiting for transfers between devices, local(): lax.all_to_all(range_part, 'col', split_axis=0, concat_axis=0, tiled=True)  18.8 us
  transfers between devices with their start and end apart: 8, of which 7 were waited for; matrix products, arithmetic and copies ran while one was open for 22% of the time, Pallas kernels for 7%

profile of v3, /device:TPU:0, one launch (start us, length us, event | category | flops | bytes accessed | tf_op | source)
XLA Modules:
  0.0 548.0 jit_solution(14455831099639849619)
XLA Ops:
  7.2 10.7 %fusion.23 = (bf16[128,29568]{1,0:T(8,128)(2,1)}, bf16[128,29568]{1,0:T(8,128)(2,1)}) fusion(bf16[256,29568]{1,0:T(8,128)(2,1)} %param.6), kind=kLoop, calls=%fused_computation.32 | loop fusion | bytes 30277632 | tf_op jit(solution)/shard_map/slice | solution.py:71
  17.9 10.5 %copy.62 = bf16[128,29568]{0,1:T(8,128)(2,1)} copy(bf16[128,29568]{1,0:T(8,128)(2,1)} %get-tuple-element.35) | data formatting | bytes 15138816
  28.3 5.2 all-to-all-start
  33.5 10.5 %copy.65 = bf16[128,29568]{0,1:T(8,128)(2,1)} copy(bf16[128,29568]{1,0:T(8,128)(2,1)} %get-tuple-element.34) | data formatting | bytes 15138816
  44.0 75.1 %all-to-all-done = bf16[8,128,3696]{1,2,0:T(8,128)(2,1)} async-done(((bf16[8,128,3696]{1,2,0:T(8,128)(2,1)}), bf16[8,128,3696]{1,2,0:T(8,128)(2,1)}, u32[]{:S(2)}, u32[]{:S(2)}) %all-to-all-start) | async-done | bytes 7569440 | tf_op jit(solution)/shard_map/all_to_all | solution.py:72
  119.1 5.0 all-to-all-start.1
  126.7 4.6 copy.49
  131.3 19.0 %copy.53 = bf16[2048,3696]{1,0:T(8,128)(2,1)} copy(bf16[2048,3696]{0,1:T(8,128)(2,1)} %param.7) | data formatting | bytes 30277632 | tf_op args[1]
  150.3 10.6 %fusion.22 = (bf16[8,128,3696]{2,1,0:T(8,128)(2,1)}, bf16[8,128,3696]{2,1,0:T(8,128)(2,1)}) fusion(bf16[8,256,3696]{2,1,0:T(8,128)(2,1)} %bitcast.36), kind=kLoop, calls=%fused_computation.31 | loop fusion | bytes 30277632 | tf_op jit(solution)/shard_map/slice | solution.py:74
  160.9 10.1 %copy.66 = bf16[8,128,3696]{1,2,0:T(8,128)(2,1)} copy(bf16[8,128,3696]{2,1,0:T(8,128)(2,1)} %get-tuple-element.32) | data formatting | bytes 15138816
  171.1 10.1 %copy.63 = bf16[8,128,3696]{1,2,0:T(8,128)(2,1)} copy(bf16[8,128,3696]{2,1,0:T(8,128)(2,1)} %get-tuple-element.33) | data formatting | bytes 15138816
  181.2 2.9 pad_maximum_fusion.3
  187.5 14.7 %convolution_bitcast_fusion.1 = f32[1152,3696]{0,1:T(8,128)} fusion(bf16[8,128,3696]{1,2,0:T(8,128)(2,1)S(1)} %copy-done.1, bf16[8,128,3696]{1,2,0:T(8,128)(2,1)} %all-to-all-done, bf16[1152,8,256]{0,2,1:T(8,128)(2,1)S(1)} %bitcast.41), kind=kOutput, calls=%fused_computation.2 | convolution fusion | flops 8735096832 | bytes 34529280 | tf_op jit(solution)/shard_map/dot_general | solution.py:77
  202.2 7.2 %all-to-all-done.1 = bf16[8,128,3696]{1,2,0:T(8,128)(2,1)} async-done(((bf16[8,128,3696]{1,2,0:T(8,128)(2,1)}), bf16[8,128,3696]{1,2,0:T(8,128)(2,1)}, u32[]{:S(2)}, u32[]{:S(2)}) %all-to-all-start.1) | async-done | bytes 7569440 | tf_op jit(solution)/shard_map/all_to_all | solution.py:72
  209.4 22.6 %fusion = f32[1152,3696]{0,1:T(8,128)} fusion(f32[1152,3696]{0,1:T(8,128)} %convolution_bitcast_fusion.1, bf16[8,128,3696]{1,2,0:T(8,128)(2,1)} %copy.66, bf16[8,128,3696]{1,2,0:T(8,128)(2,1)} %all-to-all-done.1, bf16[1152,8,256]{0,2,1:T(8,128)(2,1)} %bitcast.42), kind=kOutput, calls=%fused_computation.1 | convolution fusion | flops 8739354624 | bytes 51560448 | tf_op jit(solution)/shard_map/dot_general | solution.py:77
  232.0 10.2 %reduce-precision_convert_fusion = (bf16[768,3696]{0,1:T(8,128)(2,1)}, bf16[768,3696]{0,1:T(8,128)(2,1)}) fusion(f32[1152,3696]{0,1:T(8,128)} %fusion), kind=kLoop, calls=%fused_computation.4 | loop fusion | flops 11354112 | bytes 22708224 | tf_op jit(solution)/shard_map/convert_element_type | solution.py:85
  242.2 9.1 %fusion.5 = f32[384,1536]{1,0:T(8,128)S(1)} fusion(bf16[3696,384]{1,0:T(8,128)(2,1)S(1)} %copy-done, bf16[768,3696]{0,1:T(8,128)(2,1)} %get-tuple-element.31, bf16[768,3696]{0,1:T(8,128)(2,1)} %get-tuple-element.30), kind=kOutput, calls=%fused_computation.15 | convolution fusion | flops 4382687232 | bytes 16551936 | tf_op jit(solution)/shard_map/dot_general | solution.py:89
  251.3 15.7 %fusion.4 = f32[768,1536]{1,0:T(8,128)} fusion(bf16[768,3696]{0,1:T(8,128)(2,1)} %param.11, bf16[768,3696]{0,1:T(8,128)(2,1)} %get-tuple-element.31, bf16[768,3696]{0,1:T(8,128)(2,1)} %get-tuple-element.30), kind=kOutput, calls=%fused_computation.13 | convolution fusion | flops 8742666240 | bytes 21749760 | tf_op jit(solution)/shard_map/dot_general | solution.py:86
  272.0 4.7 all-to-all-start.2
  276.7 8.4 %fusion.12 = bf16[8,128,384]{2,1,0:T(8,128)(2,1)S(1)} fusion(bf16[3696,384]{1,0:T(8,128)(2,1)S(1)} %copy-done, bf16[8,128,3696]{1,2,0:T(8,128)(2,1)} %copy.66, bf16[8,128,3696]{1,2,0:T(8,128)(2,1)} %all-to-all-done.1), kind=kOutput, calls=%fused_computation.24 | convolution fusion | flops 2922184704 | bytes 18763776 | tf_op jit(solution)/shard_map/dot_general | solution.py:80
  285.2 8.4 %fusion.15 = bf16[8,128,384]{2,1,0:T(8,128)(2,1)S(1)} fusion(bf16[3696,384]{1,0:T(8,128)(2,1)S(1)} %copy-done, bf16[8,128,3696]{1,2,0:T(8,128)(2,1)} %copy.63, bf16[8,128,3696]{1,2,0:T(8,128)(2,1)} %all-to-all-done), kind=kOutput, calls=%fused_computation.25 | convolution fusion | flops 2922184704 | bytes 18763776 | tf_op jit(solution)/shard_map/dot_general | solution.py:80
  294.9 23.9 %all-to-all-done.2 = f32[8,144,768]{2,1,0:T(8,128)} async-done(((f32[8,144,768]{2,1,0:T(8,128)}), f32[8,144,768]{2,1,0:T(8,128)}, u32[]{:S(2)}, u32[]{:S(2)}) %all-to-all-start.2) | async-done | bytes 3538976 | tf_op jit(solution)/shard_map/all_to_all | solution.py:98
  318.8 3.0 reduce_sum.21
  321.9 37.7 %all-reduce.4.cloned.1.call-done = f32[144,768]{1,0:T(8,128)} async-done(((f32[144,768]{1,0:T(8,128)}), f32[144,768]{1,0:T(8,128)}) %all-reduce.4.cloned.1.call-update) | async-done | bytes 442384 | tf_op jit(solution)/shard_map/psum | solution.py:101
  361.1 4.3 all-to-all-start.3
  365.5 4.5 slice.87
  370.0 18.8 %all-to-all-done.3 = bf16[8,256,384]{2,1,0:T(8,128)(2,1)} async-done(((bf16[8,256,384]{2,1,0:T(8,128)(2,1)}), bf16[8,256,384]{2,1,0:T(8,128)(2,1)}, u32[]{:S(2)}, u32[]{:S(2)}) %all-to-all-start.3) | async-done | bytes 1572896 | tf_op jit(solution)/shard_map/all_to_all | solution.py:105
  395.6 3.7 fusion.24.gram_ref
  399.3 36.5 %shard_map.85 = f32[384,128]{1,0:T(8,128)S(1)} custom-call(f32[384,384]{1,0:T(8,128)S(1)} %fusion.24.gram_ref, f32[384,128]{1,0:T(8,128)S(1)} %pad.4.right_ref), custom_call_target="tpu_custom_call" | custom-call | tf_op jit(solution)/shard_map/pallas_call | solution.py:49
  436.6 3.3 convert_element_type.44
  439.9 96.5 %all-reduce.6.cloned.1.call-done = bf16[384,3696]{0,1:T(8,128)(2,1)} async-done(((bf16[384,3696]{0,1:T(8,128)(2,1)}), bf16[384,3696]{0,1:T(8,128)(2,1)}) %all-reduce.6.cloned.1.call-update) | async-done | bytes 2838544 | tf_op jit(solution)/shard_map/psum | solution.py:104
  536.4 4.7 convert_element_type.45
  (28 shorter events, 21.4 us)
Async XLA Ops:
  7.2 235.0 %copy-start = (bf16[3696,384]{1,0:T(8,128)(2,1)S(1)}, bf16[3696,384]{1,0:T(8,128)(2,1)}, u32[]{:S(2)}) copy-start(bf16[3696,384]{1,0:T(8,128)(2,1)} %param.8) | copy-start | bytes 8515588
  28.3 90.8 %all-to-all-start = ((bf16[8,128,3696]{1,2,0:T(8,128)(2,1)}), bf16[8,128,3696]{1,2,0:T(8,128)(2,1)}, u32[]{:S(2)}, u32[]{:S(2)}) async-start(bf16[8,128,3696]{1,2,0:T(8,128)(2,1)} %bitcast.38), calls=%async_computation | async-start | bytes 15138816 | tf_op jit(solution)/shard_map/all_to_all | solution.py:72
  119.1 90.3 %all-to-all-start.1 = ((bf16[8,128,3696]{1,2,0:T(8,128)(2,1)}), bf16[8,128,3696]{1,2,0:T(8,128)(2,1)}, u32[]{:S(2)}, u32[]{:S(2)}) async-start(bf16[8,128,3696]{1,2,0:T(8,128)(2,1)} %bitcast.37), calls=%async_computation.1 | async-start | bytes 15138816 | tf_op jit(solution)/shard_map/all_to_all | solution.py:72
  181.2 6.2 %copy-start.1 = (bf16[8,128,3696]{1,2,0:T(8,128)(2,1)S(1)}, bf16[8,128,3696]{1,2,0:T(8,128)(2,1)}, u32[]{:S(2)}) copy-start(bf16[8,128,3696]{1,2,0:T(8,128)(2,1)} %copy.63) | copy-start | bytes 22708228
  184.1 2.4 copy-start.2
  272.0 46.8 %all-to-all-start.2 = ((f32[8,144,768]{2,1,0:T(8,128)}), f32[8,144,768]{2,1,0:T(8,128)}, u32[]{:S(2)}, u32[]{:S(2)}) async-start(f32[8,144,768]{2,1,0:T(8,128)} %pad_maximum_fusion.6), calls=%async_computation.2 | async-start | bytes 7077888 | tf_op jit(solution)/shard_map/all_to_all | solution.py:98
  276.7 82.8 %all-reduce.4.cloned.1.call-start = ((), (), s32[]{:S(2)}) async-start(), calls=%async_computation.4 | async-start | bytes 884736 | tf_op jit(solution)/shard_map/psum | solution.py:101
  321.8 70.8 %all-gather.3.cloned.1.call-start = ((), (), s32[]{:S(2)}) async-start(), calls=%async_computation.5 | async-start | bytes 1327104 | tf_op jit(solution)/shard_map/all_gather | solution.py:102
  361.1 27.8 %all-to-all-start.3 = ((bf16[8,256,384]{2,1,0:T(8,128)(2,1)}), bf16[8,256,384]{2,1,0:T(8,128)(2,1)}, u32[]{:S(2)}, u32[]{:S(2)}) async-start(bf16[8,256,384]{2,1,0:T(8,128)(2,1)} %pad_maximum_fusion.9), calls=%async_computation.3 | async-start | bytes 3145728 | tf_op jit(solution)/shard_map/all_to_all | solution.py:105
  365.4 27.8 %copy-start.3 = (f32[144,768]{1,0:T(8,128)S(1)}, f32[144,768]{1,0:T(8,128)}, u32[]{:S(2)}) copy-start(f32[144,768]{1,0:T(8,128)} %all-reduce.4.cloned.1.call-done) | copy-start | bytes 1327108
  365.5 71.2 %all-gather.5.cloned.1.call-start = ((), (), s32[]{:S(2)}) async-start(), calls=%async_computation.6 | async-start | bytes 1769472 | tf_op jit(solution)/shard_map/all_gather | solution.py:108
  392.7 143.7 %all-reduce.6.cloned.1.call-start = ((), (), s32[]{:S(2)}) async-start(), calls=%async_computation.7 | async-start | bytes 5677056 | tf_op jit(solution)/shard_map/psum | solution.py:104
Sparse Core Ops, SparseCore 0:
  321.9 37.5 all-reduce.3
  362.1 30.4 all-gather.2
  395.3 26.6 all-gather.4
  424.9 111.3 all-reduce.5
